TPU v7x, 256 devices: a whole 4x4x8 slice. The times are simulated.
256 devices in a mesh: dp: 4 (over x), ep: 64 (over y, z, core).
Axes of the slice: x: 4, y: 4, z: 8, core: 2. Of those that a mesh axis runs over, the one named last changes fastest.
Arguments:
- tokens: bfloat16 [4, 2048, 2048], P('dp', 'ep'), may hold values from -12 to 12
- cotangent: bfloat16 [4, 2048, 2048], P('dp', 'ep'), may hold values from -6 to 6
- assign: int32 [4, 2048, 8], P('dp', 'ep'), may hold values from 0 to 63, as said below
- w_router: bfloat16 [2048, 64], replicated, may hold values from -0.125 to 0.125
- w_gate: bfloat16 [64, 2048, 768], P('ep'), may hold values from -0.125 to 0.125
- w_up: bfloat16 [64, 2048, 768], P('ep'), may hold values from -0.125 to 0.125
- w_down: bfloat16 [64, 2048, 768], P('ep'), may hold values from -0.21875 to 0.21875
Outputs:
- grad_tokens: bfloat16 [4, 2048, 2048], P('dp', 'ep')
- grad_router: float32 [2048, 64], replicated
- grad_gate: bfloat16 [64, 2048, 768], P('ep', 'dp')
- grad_up: bfloat16 [64, 2048, 768], P('ep', 'dp')
- grad_down: bfloat16 [64, 2048, 768], P('ep', 'dp')
Inputs may be any that keep to these rules, and one draw needn't show every extreme that they name: `assign`: each token names 8 different experts; the routes of the 32 tokens of one device name one expert at most 8 times, and in every draw one expert is named exactly 8 times by the routes of every device.
All inputs are finite; a program needn't handle non-finite values.
Results may differ from a plain program's by a relative error of at most 0.015.
Values may be sent and summed in bfloat16 or wider, within the bound.
A program may use at most 128 MiB of HBM per device.

v0:
```python
import jax
import jax.numpy as jnp
from jax import lax
from jax.sharding import PartitionSpec as P

ITERS = 3
cos_scale = 48.0
eps_norm = 1e-06
contract_first = (((0,), (0,)), ((), ()))
contract_last = (((1,), (1,)), ((), ()))


def logit_map(flat_tokens, router):
    inner_products = jnp.dot(flat_tokens, router, precision=lax.Precision.HIGHEST)
    token_norm = jnp.sqrt(jnp.sum(flat_tokens * flat_tokens, axis=1) + eps_norm)
    column_norm = jnp.sqrt(jnp.sum(router * router, axis=0) + eps_norm)
    return cos_scale * inner_products / (token_norm[:, None] * column_norm[None, :])


def expert_backward(expert_rows, expert_cotangent, rows_gate, gate_matrix, up_matrix, down_matrix):
    gate_linear = jnp.dot(expert_rows, gate_matrix, preferred_element_type=jnp.float32)
    up_linear = jnp.dot(expert_rows, up_matrix, preferred_element_type=jnp.float32)
    sigmoid_gate = jax.nn.sigmoid(gate_linear)
    activation = gate_linear * sigmoid_gate
    product = activation * up_linear
    hidden = product.astype(jnp.bfloat16)
    weighted = (rows_gate[:, None] * product).astype(jnp.bfloat16)
    raw_back = jnp.dot(expert_cotangent, down_matrix, preferred_element_type=jnp.float32)
    gate_grad = jnp.sum(raw_back * hidden.astype(jnp.float32), axis=1).astype(jnp.bfloat16)
    scaled_back = rows_gate[:, None] * raw_back
    up_delta = (scaled_back * activation).astype(jnp.bfloat16)
    gate_delta = (
        scaled_back * up_linear * sigmoid_gate * (1.0 + gate_linear * (1.0 - sigmoid_gate))
    ).astype(jnp.bfloat16)
    route_back = (
        lax.dot_general(gate_delta, gate_matrix, contract_last, preferred_element_type=jnp.float32)
        + lax.dot_general(up_delta, up_matrix, contract_last, preferred_element_type=jnp.float32)
    ).astype(jnp.bfloat16)
    return (gate_grad, route_back, gate_delta, up_delta, weighted)


def column_sums(values):
    return lax.psum(jnp.sum(values, axis=0), "ep")


def per_device(tokens, cotangent, assign, w_router, w_gate, w_up, w_down):
    local_tokens = tokens[0]
    local_cotangent = cotangent[0]
    route_ids = assign[0]
    token_count, per_token = route_ids.shape
    model_width = local_tokens.shape[1]
    experts = w_router.shape[1]
    slot_cap = min(token_count, 2 * token_count * per_token // experts)
    logits, logit_vjp = jax.vjp(
        logit_map, local_tokens.astype(jnp.float32), w_router.astype(jnp.float32)
    )
    kernel_start = jnp.exp(logits)
    kernel = kernel_start
    saved_steps = []
    for sweep_index in range(ITERS):
        column = column_sums(kernel)
        scaled = kernel / column[None, :]
        row_total = jnp.sum(scaled, axis=1, keepdims=True)
        kernel = scaled / row_total
        saved_steps.append((column, scaled, row_total, kernel))
    expert_ids = jnp.arange(experts, dtype=jnp.int32)
    onehot = (route_ids[:, :, None] == expert_ids).astype(jnp.float32)
    picked = jnp.sum(onehot * kernel[:, None, :], axis=2)
    picked_sum = jnp.sum(picked, axis=1, keepdims=True)
    gates = picked / picked_sum
    gate_half = gates.astype(jnp.bfloat16)
    flat_route = route_ids.reshape(-1)
    member = (flat_route[:, None] == expert_ids).astype(jnp.int32)
    earlier = jnp.cumsum(member, axis=0) - member
    slot_index = jnp.sum(earlier * member, axis=1)
    target = flat_route * slot_cap + slot_index
    route_slots = (
        jnp.arange(experts * slot_cap, dtype=jnp.int32)[:, None] == target[None, :]
    ).astype(jnp.bfloat16)
    token_slots = jnp.sum(route_slots.reshape(experts * slot_cap, token_count, per_token), axis=2)
    send_tokens = jnp.dot(token_slots, local_tokens, preferred_element_type=jnp.float32).astype(
        jnp.bfloat16
    )
    send_cotangent = jnp.dot(
        token_slots, local_cotangent, preferred_element_type=jnp.float32
    ).astype(jnp.bfloat16)
    send_gate = jnp.dot(
        route_slots, gate_half.reshape(-1), preferred_element_type=jnp.float32
    ).astype(jnp.bfloat16)
    recv_tokens, recv_cotangent, recv_gate = (
        lax.all_to_all(
            send_tokens.reshape(experts, slot_cap, model_width),
            "ep",
            split_axis=0,
            concat_axis=0,
            tiled=True,
        ),
        lax.all_to_all(
            send_cotangent.reshape(experts, slot_cap, model_width),
            "ep",
            split_axis=0,
            concat_axis=0,
            tiled=True,
        ),
        lax.all_to_all(
            send_gate.reshape(experts, slot_cap), "ep", split_axis=0, concat_axis=0, tiled=True
        ),
    )
    expert_rows = recv_tokens.reshape(-1, model_width)
    expert_cotangent = recv_cotangent.reshape(-1, model_width)
    rows_gate = recv_gate.reshape(-1).astype(jnp.float32)
    gate_grad, route_back, gate_delta, up_delta, weighted = expert_backward(
        expert_rows, expert_cotangent, rows_gate, w_gate[0], w_up[0], w_down[0]
    )
    back_rows, back_gate = (
        lax.all_to_all(
            route_back.reshape(experts, slot_cap, model_width),
            "ep",
            split_axis=0,
            concat_axis=0,
            tiled=True,
        ),
        lax.all_to_all(
            gate_grad.reshape(experts, slot_cap), "ep", split_axis=0, concat_axis=0, tiled=True
        ),
    )
    expert_back = lax.dot_general(
        token_slots,
        back_rows.reshape(-1, model_width),
        contract_first,
        preferred_element_type=jnp.float32,
    )
    route_grad = lax.dot_general(
        route_slots, back_gate.reshape(-1), contract_first, preferred_element_type=jnp.float32
    ).reshape(token_count, per_token)
    hidden_units = gate_delta.shape[1]
    summed = lax.psum_scatter(
        jnp.concatenate(
            [
                lax.dot_general(
                    expert_rows, gate_delta, contract_first, preferred_element_type=jnp.float32
                ),
                lax.dot_general(
                    expert_rows, up_delta, contract_first, preferred_element_type=jnp.float32
                ),
                lax.dot_general(
                    expert_cotangent, weighted, contract_first, preferred_element_type=jnp.float32
                ),
            ],
            axis=1,
        ).astype(jnp.bfloat16),
        "dp",
        scatter_dimension=0,
        tiled=True,
    ).astype(jnp.float32)
    grad_gate = summed[:, :hidden_units]
    grad_up = summed[:, hidden_units : 2 * hidden_units]
    grad_down = summed[:, 2 * hidden_units :]
    picked_grad = (route_grad - jnp.sum(route_grad * gates, axis=1, keepdims=True)) / picked_sum
    kernel_grad = jnp.sum(onehot * picked_grad[:, :, None], axis=1)
    for sweep_index in reversed(range(ITERS)):
        column, scaled, row_total, kernel_step = saved_steps[sweep_index]
        scaled_grad = (
            kernel_grad - jnp.sum(kernel_grad * kernel_step, axis=1, keepdims=True)
        ) / row_total
        moment = lax.psum(jnp.sum(scaled_grad * scaled, axis=0), "ep")
        kernel_grad = (scaled_grad - moment[None, :]) / column[None, :]
    logit_grad = kernel_grad * kernel_start
    router_back, router_part = logit_vjp(logit_grad)
    grad_router = lax.psum(router_part, ("dp", "ep"))
    grad_tokens = (expert_back + router_back).astype(jnp.bfloat16)[None]
    return (
        grad_tokens,
        grad_router,
        grad_gate.astype(jnp.bfloat16)[None],
        grad_up.astype(jnp.bfloat16)[None],
        grad_down.astype(jnp.bfloat16)[None],
    )


def solution(mesh):
    return jax.shard_map(
        per_device,
        mesh=mesh,
        in_specs=(
            P("dp", "ep", None),
            P("dp", "ep", None),
            P("dp", "ep", None),
            P(),
            P("ep", None, None),
            P("ep", None, None),
            P("ep", None, None),
        ),
        out_specs=(
            P("dp", "ep", None),
            P(),
            P("ep", "dp", None),
            P("ep", "dp", None),
            P("ep", "dp", None),
        ),
        check_vma=False,
    )
```

profile of v0, /device:TPU:2, one launch (start us, length us, event | category | flops | bytes accessed | tf_op | source)
XLA Modules:
  0.0 1251.3 jit_solution(17761611733418999477)
XLA Ops:
  15.1 131.8 %psum.49 = f32[64]{0:T(128)S(1)} all-reduce(f32[64]{0:T(128)S(1)} %get-tuple-element.33), channel_id=1, replica_groups=mesh['dp'=4,'ep'=64] {'ep'}, use_global_device_ids=true, to_apply=%region_7.0 | all-reduce | flops 64 | bytes 512 | tf_op jit(solution)/shard_map/psum | solution.py:43
  147.1 124.1 %psum.50 = f32[64]{0:T(128)S(1)} all-reduce(f32[64]{0:T(128)S(1)} %fusion.67), channel_id=1, replica_groups=mesh['dp'=4,'ep'=64] {'ep'}, use_global_device_ids=true, to_apply=%region_10.0 | all-reduce | flops 64 | bytes 512 | tf_op jit(solution)/shard_map/psum | solution.py:43
  271.4 124.0 %psum.51 = f32[64]{0:T(128)S(1)} all-reduce(f32[64]{0:T(128)S(1)} %fusion.73), channel_id=1, replica_groups=mesh['dp'=4,'ep'=64] {'ep'}, use_global_device_ids=true, to_apply=%region_13.0 | all-reduce | flops 64 | bytes 512 | tf_op jit(solution)/shard_map/psum | solution.py:43
  398.9 4.6 all-to-all-start
  406.9 6.1 all-to-all-done
  413.0 5.6 all-to-all-start.2
  420.6 49.0 %all-to-all-done.2 = bf16[64,8,2048]{2,1,0:T(8,128)(2,1)} async-done(((bf16[64,8,2048]{2,1,0:T(8,128)(2,1)}), bf16[64,8,2048]{2,1,0:T(8,128)(2,1)}, u32[]{:S(2)}, u32[]{:S(2)}) %all-to-all-start.2) | async-done | bytes 2097184 | tf_op jit(solution)/shard_map/all_to_all | solution.py:91
  469.6 6.1 all-to-all-start.1
  476.1 5.5 fusion.6
  481.6 4.6 fusion.2
  486.2 40.5 %all-to-all-done.1 = bf16[64,8,2048]{2,1,0:T(8,128)(2,1)} async-done(((bf16[64,8,2048]{2,1,0:T(8,128)(2,1)}), bf16[64,8,2048]{2,1,0:T(8,128)(2,1)}, u32[]{:S(2)}, u32[]{:S(2)}) %all-to-all-start.1) | async-done | bytes 2097184 | tf_op jit(solution)/shard_map/all_to_all | solution.py:98
  526.7 4.6 convolution_convert_fusion
  531.4 4.0 multiply_reduce_fusion
  535.4 4.0 convolution_convert_fusion.1
  539.5 3.4 convolution_convert_fusion.2
  542.9 4.5 pad_maximum_fusion
  548.1 6.4 all-to-all-start.4
  554.5 3.3 fusion
  557.8 3.1 fusion.14
  563.5 7.7 all-to-all-start.3
  580.8 155.9 %psum.52 = f32[64]{0:T(128)} all-reduce(f32[64]{0:T(128)} %multiply_reduce_fusion.7), channel_id=1, replica_groups=mesh['dp'=4,'ep'=64] {'ep'}, use_global_device_ids=true, to_apply=%region_22.23 | all-reduce | flops 64 | bytes 512 | tf_op jit(solution)/shard_map/psum | solution.py:166
  739.6 124.5 %psum.53 = f32[64]{0:T(128)} all-reduce(f32[64]{0:T(128)} %get-tuple-element.31), channel_id=1, replica_groups=mesh['dp'=4,'ep'=64] {'ep'}, use_global_device_ids=true, to_apply=%region_25.26 | all-reduce | flops 64 | bytes 512 | tf_op jit(solution)/shard_map/psum | solution.py:166
  866.9 124.7 %psum.54 = f32[64]{0:T(128)} all-reduce(f32[64]{0:T(128)} %multiply_reduce_fusion.3), channel_id=1, replica_groups=mesh['dp'=4,'ep'=64] {'ep'}, use_global_device_ids=true, to_apply=%region_28.29 | all-reduce | flops 64 | bytes 512 | tf_op jit(solution)/shard_map/psum | solution.py:166
  1010.7 231.3 %all-reduce.2.cloned.1.call-done = f32[2048,64]{0,1:T(8,128)} async-done(((f32[2048,64]{0,1:T(8,128)}), f32[2048,64]{0,1:T(8,128)}) %all-reduce.2.cloned.1.call-update) | async-done | bytes 524304 | tf_op jit(solution)/shard_map/psum | solution.py:170
  (134 shorter events, 56.1 us)
Async XLA Ops:
  8.0 473.6 %copy-start = (bf16[1,2048,768]{2,1,0:T(8,128)(2,1)S(1)}, bf16[1,2048,768]{2,1,0:T(8,128)(2,1)}, u32[]{:S(2)}) copy-start(bf16[1,2048,768]{2,1,0:T(8,128)(2,1)} %param.11) | copy-start | bytes 9437188
  8.9 404.0 %copy-start.3 = (s32[1,32,8]{2,1,0:T(8,128)}, s32[1,32,8]{2,1,0:T(8,128)S(1)}, u32[]{:S(2)}) copy-start(s32[1,32,8]{2,1,0:T(8,128)S(1)} %copy.33) | copy-start | bytes 3076
  11.6 3.5 copy-start.16
  146.9 257.0 %copy-start.10 = (f32[64]{0:T(128)}, f32[64]{0:T(128)S(1)}, u32[]{:S(2)}) copy-start(f32[64]{0:T(128)S(1)} %psum.49) | copy-start | bytes 772
  147.0 256.9 %copy-start.11 = (f32[32]{0:T(128)}, f32[32]{0:T(128)S(1)}, u32[]{:S(2)}) copy-start(f32[32]{0:T(128)S(1)} %fusion.65) | copy-start | bytes 388
  271.2 132.7 %copy-start.12 = (f32[64]{0:T(128)}, f32[64]{0:T(128)S(1)}, u32[]{:S(2)}) copy-start(f32[64]{0:T(128)S(1)} %psum.50) | copy-start | bytes 772
  271.3 132.6 %copy-start.13 = (f32[32]{0:T(128)}, f32[32]{0:T(128)S(1)}, u32[]{:S(2)}) copy-start(f32[32]{0:T(128)S(1)} %fusion.70) | copy-start | bytes 388
  396.8 7.2 copy-start.21
  398.9 14.0 %all-to-all-start = ((bf16[64,1,8]{2,1,0:T(2,128)(2,1)}), bf16[64,1,8]{2,1,0:T(2,128)(2,1)S(1)}, u32[]{:S(2)}, u32[]{:S(2)}) async-start(bf16[64,1,8]{2,1,0:T(2,128)(2,1)} %all_to_all.25), calls=%async_computation | async-start | bytes 65536 | tf_op jit(solution)/shard_map/all_to_all | solution.py:105
  403.9 14.6 %copy-start.4 = (bf16[512,32]{0,1:T(8,128)(2,1)}, bf16[512,32]{0,1:T(8,128)(2,1)S(1)}, u32[]{:S(2)}) copy-start(bf16[512,32]{0,1:T(8,128)(2,1)S(1)} %fusion.41) | copy-start | bytes 98308
  406.9 11.7 copy-start.9
  413.0 56.6 %all-to-all-start.2 = ((bf16[64,8,2048]{2,1,0:T(8,128)(2,1)}), bf16[64,8,2048]{2,1,0:T(8,128)(2,1)}, u32[]{:S(2)}, u32[]{:S(2)}) async-start(bf16[64,8,2048]{2,1,0:T(8,128)(2,1)} %fusion.13), calls=%async_computation.2 | async-start | bytes 4194304 | tf_op jit(solution)/shard_map/all_to_all | solution.py:91
  469.6 57.2 %all-to-all-start.1 = ((bf16[64,8,2048]{2,1,0:T(8,128)(2,1)}), bf16[64,8,2048]{2,1,0:T(8,128)(2,1)}, u32[]{:S(2)}, u32[]{:S(2)}) async-start(bf16[64,8,2048]{2,1,0:T(8,128)(2,1)} %fusion.12), calls=%async_computation.1 | async-start | bytes 4194304 | tf_op jit(solution)/shard_map/all_to_all | solution.py:98
  475.7 525.0 %reduce-scatter.2.cloned.1.call-start = ((), (), s32[]{:S(2)}) async-start(), calls=%async_computation.7 | async-start | bytes 11796480 | tf_op jit(solution)/shard_map/reduce_scatter | solution.py:137
  526.7 4.6 copy-start.27
  526.7 4.7 copy-start.32
  526.7 4.7 copy-start.33
  535.4 4.0 copy-start.29
  535.4 4.0 copy-start.31
  548.1 15.4 %all-to-all-start.4 = ((bf16[64,1,8]{2,1,0:T(2,128)(2,1)}), bf16[64,1,8]{2,1,0:T(2,128)(2,1)}, u32[]{:S(2)}, u32[]{:S(2)}) async-start(bf16[64,1,8]{2,1,0:T(2,128)(2,1)} %convert_element_type.108), calls=%async_computation.4 | async-start | bytes 65536 | tf_op jit(solution)/shard_map/all_to_all | solution.py:123
  560.9 433.5 %copy-start.1 = (bf16[2048,64]{0,1:T(8,128)(2,1)S(1)}, bf16[2048,64]{0,1:T(8,128)(2,1)}, u32[]{:S(2)}) copy-start(bf16[2048,64]{0,1:T(8,128)(2,1)} %param.10) | copy-start | bytes 786436
  560.9 433.5 %copy-start.2 = (bf16[1,32,2048]{2,1,0:T(8,128)(2,1)S(1)}, bf16[1,32,2048]{2,1,0:T(8,128)(2,1)}, u32[]{:S(2)}) copy-start(bf16[1,32,2048]{2,1,0:T(8,128)(2,1)} %param.7) | copy-start | bytes 393220
  563.5 434.1 %all-to-all-start.3 = ((bf16[64,8,2048]{2,1,0:T(8,128)(2,1)}), bf16[64,8,2048]{2,1,0:T(8,128)(2,1)}, u32[]{:S(2)}, u32[]{:S(2)}) async-start(bf16[64,8,2048]{2,1,0:T(8,128)(2,1)} %fusion.14), calls=%async_computation.3 | async-start | bytes 4194304 | tf_op jit(solution)/shard_map/all_to_all | solution.py:116
  571.2 670.8 %all-reduce.2.cloned.1.call-start = ((), (), s32[]{:S(2)}) async-start(), calls=%async_computation.6 | async-start | bytes 1048576 | tf_op jit(solution)/shard_map/psum | solution.py:170
  (17 other events, 26.2 us)
Sparse Core Ops, SparseCore 0:
  547.5 87.0 reduce-scatter.1
Sparse Core Ops, SparseCore 1:
  996.5 245.4 all-reduce.1
where the time goes:
time: 1250 us
  blocking collectives  785 us (63%)
  waiting for transfers between devices  330 us (26%)
  matrix products  46 us (4%)
  starting transfers between devices  30.6 us (2%)
  other arithmetic  24.4 us (2%)
  local copies, waits for them, and re-layouts  19.8 us (2%)
  between operations  16 us (1%)
    psum x3, blocking collectives, per_device(): moment = lax.psum(jnp.sum(scaled_grad * scaled, axis=0), 'ep')  405 us
    psum x3, blocking collectives, column_sums(): return lax.psum(jnp.sum(values, axis=0), 'ep')  380 us
    psum x1, waiting for transfers between devices, per_device(): grad_router = lax.psum(router_part, ('dp', 'ep'))  231 us
    all_to_all x1, waiting for transfers between devices, per_device(): lax.all_to_all(send_tokens.reshape(experts, slot_cap, model_width), 'ep',...  49 us
    all_to_all x1, waiting for transfers between devices, per_device(): lax.all_to_all(send_cotangent.reshape(experts, slot_cap, model_width), 'e...  40.5 us
  transfers between devices with their start and end apart: 7, of which 5 were waited for; matrix products, arithmetic and copies ran while one was open for 4% of the time, Pallas kernels for 0%

commit v1 on v0

--- a/solution.py
+++ b/solution.py
@@ -167,7 +167,7 @@
         kernel_grad = (scaled_grad - moment[None, :]) / column[None, :]
     logit_grad = kernel_grad * kernel_start
     router_back, router_part = logit_vjp(logit_grad)
-    grad_router = lax.psum(router_part, ("dp", "ep"))
+    grad_router = lax.psum(lax.psum(router_part, "ep"), "dp")
     grad_tokens = (expert_back + router_back).astype(jnp.bfloat16)[None]
     return (
         grad_tokens,

time: 1250 us -> 1200 us (0.960)
  waiting for transfers between devices: 330 us -> 293 us
  blocking collectives: 785 us -> 758 us
    psum x1 -> x2, waiting for transfers between devices: 231 us -> 197 us  [per_device(): grad_router = lax.psum(lax.psum(router_part, 'ep'), 'dp')]
    psum x3, blocking collectives: 405 us -> 378 us  [per_device(): moment = lax.psum(jnp.sum(scaled_grad * scaled, axis=0), 'ep')]
  transfers between devices with their start and end apart: 7 -> 8, of which waited for: 5 -> 5; matrix products, arithmetic and copies ran while one was open for 4% -> 5% of each run, Pallas kernels for 0% -> 0%
where the time goes in v1:
time: 1200 us
  blocking collectives  758 us (63%)
  waiting for transfers between devices  293 us (24%)
  matrix products  53.2 us (4%)
  starting transfers between devices  28.1 us (2%)
  other arithmetic  27.6 us (2%)
  local copies, waits for them, and re-layouts  19.2 us (2%)
  between operations  16 us (1%)
    psum x3, blocking collectives, column_sums(): return lax.psum(jnp.sum(values, axis=0), 'ep')  380 us
    psum x3, blocking collectives, per_device(): moment = lax.psum(jnp.sum(scaled_grad * scaled, axis=0), 'ep')  378 us
    psum x2, waiting for transfers between devices, per_device(): grad_router = lax.psum(lax.psum(router_part, 'ep'), 'dp')  197 us
    all_to_all x1, waiting for transfers between devices, per_device(): lax.all_to_all(send_tokens.reshape(experts, slot_cap, model_width), 'ep',...  49 us
    all_to_all x1, waiting for transfers between devices, per_device(): lax.all_to_all(send_cotangent.reshape(experts, slot_cap, model_width), 'e...  40.8 us
  transfers between devices with their start and end apart: 8, of which 5 were waited for; matrix products, arithmetic and copies ran while one was open for 5% of the time, Pallas kernels for 0%

profile of v1, /device:TPU:2, one launch (start us, length us, event | category | flops | bytes accessed | tf_op | source)
XLA Modules:
  0.0 1195.3 jit_solution(728975241598417634)
XLA Ops:
  14.5 131.8 %psum.56 = f32[64]{0:T(128)S(1)} all-reduce(f32[64]{0:T(128)S(1)} %get-tuple-element.33), channel_id=1, replica_groups=mesh['dp'=4,'ep'=64] {'ep'}, use_global_device_ids=true, to_apply=%region_7.0 | all-reduce | flops 64 | bytes 512 | tf_op jit(solution)/shard_map/psum | solution.py:43
  146.5 124.1 %psum.57 = f32[64]{0:T(128)S(1)} all-reduce(f32[64]{0:T(128)S(1)} %fusion.67), channel_id=1, replica_groups=mesh['dp'=4,'ep'=64] {'ep'}, use_global_device_ids=true, to_apply=%region_10.0 | all-reduce | flops 64 | bytes 512 | tf_op jit(solution)/shard_map/psum | solution.py:43
  270.9 124.0 %psum.58 = f32[64]{0:T(128)S(1)} all-reduce(f32[64]{0:T(128)S(1)} %fusion.73), channel_id=1, replica_groups=mesh['dp'=4,'ep'=64] {'ep'}, use_global_device_ids=true, to_apply=%region_13.0 | all-reduce | flops 64 | bytes 512 | tf_op jit(solution)/shard_map/psum | solution.py:43
  398.3 4.6 all-to-all-start
  406.3 6.1 all-to-all-done
  412.4 5.6 all-to-all-start.2
  420.0 49.0 %all-to-all-done.2 = bf16[64,8,2048]{2,1,0:T(8,128)(2,1)} async-done(((bf16[64,8,2048]{2,1,0:T(8,128)(2,1)}), bf16[64,8,2048]{2,1,0:T(8,128)(2,1)}, u32[]{:S(2)}, u32[]{:S(2)}) %all-to-all-start.2) | async-done | bytes 2097184 | tf_op jit(solution)/shard_map/all_to_all | solution.py:91
  468.9 6.1 all-to-all-start.1
  475.3 5.5 fusion.6
  480.7 4.6 fusion.2
  485.4 40.8 %all-to-all-done.1 = bf16[64,8,2048]{2,1,0:T(8,128)(2,1)} async-done(((bf16[64,8,2048]{2,1,0:T(8,128)(2,1)}), bf16[64,8,2048]{2,1,0:T(8,128)(2,1)}, u32[]{:S(2)}, u32[]{:S(2)}) %all-to-all-start.1) | async-done | bytes 2097184 | tf_op jit(solution)/shard_map/all_to_all | solution.py:98
  526.1 6.9 multiply_reduce_fusion
  533.7 6.1 all-to-all-start.4
  539.9 6.2 convolution_convert_fusion
  546.1 5.2 convolution_convert_fusion.1
  551.3 5.2 convolution_convert_fusion.2
  566.0 129.4 %psum.59 = f32[64]{0:T(128)} all-reduce(f32[64]{0:T(128)} %multiply_reduce_fusion.7), channel_id=1, replica_groups=mesh['dp'=4,'ep'=64] {'ep'}, use_global_device_ids=true, to_apply=%region_22.23 | all-reduce | flops 64 | bytes 512 | tf_op jit(solution)/shard_map/psum | solution.py:166
  698.3 124.6 %psum.60 = f32[64]{0:T(128)} all-reduce(f32[64]{0:T(128)} %get-tuple-element.31), channel_id=1, replica_groups=mesh['dp'=4,'ep'=64] {'ep'}, use_global_device_ids=true, to_apply=%region_25.26 | all-reduce | flops 64 | bytes 512 | tf_op jit(solution)/shard_map/psum | solution.py:166
  825.6 124.5 %psum.61 = f32[64]{0:T(128)} all-reduce(f32[64]{0:T(128)} %multiply_reduce_fusion.3), channel_id=1, replica_groups=mesh['dp'=4,'ep'=64] {'ep'}, use_global_device_ids=true, to_apply=%region_28.29 | all-reduce | flops 64 | bytes 512 | tf_op jit(solution)/shard_map/psum | solution.py:166
  955.0 7.7 pad_maximum_fusion
  965.9 3.1 fusion.14
  969.0 5.6 all-to-all-start.3
  975.8 165.6 %all-reduce.3.cloned.1.call-done = f32[2048,64]{0,1:T(8,128)} async-done(((f32[2048,64]{0,1:T(8,128)}), f32[2048,64]{0,1:T(8,128)}) %all-reduce.3.cloned.1.call-update) | async-done | bytes 524304 | tf_op jit(solution)/shard_map/psum | solution.py:170
  1154.6 31.4 %all-reduce.5.cloned.1.call-done = f32[2048,64]{0,1:T(8,128)} async-done(((f32[2048,64]{0,1:T(8,128)}), f32[2048,64]{0,1:T(8,128)}) %all-reduce.5.cloned.1.call-update) | async-done | bytes 524304 | tf_op jit(solution)/shard_map/psum | solution.py:170
  (131 shorter events, 55.9 us)
Async XLA Ops:
  8.0 472.7 %copy-start = (bf16[1,2048,768]{2,1,0:T(8,128)(2,1)S(1)}, bf16[1,2048,768]{2,1,0:T(8,128)(2,1)}, u32[]{:S(2)}) copy-start(bf16[1,2048,768]{2,1,0:T(8,128)(2,1)} %param.11) | copy-start | bytes 9437188
  8.9 403.4 %copy-start.3 = (s32[1,32,8]{2,1,0:T(8,128)}, s32[1,32,8]{2,1,0:T(8,128)S(1)}, u32[]{:S(2)}) copy-start(s32[1,32,8]{2,1,0:T(8,128)S(1)} %copy.33) | copy-start | bytes 3076
  146.3 256.9 %copy-start.10 = (f32[64]{0:T(128)}, f32[64]{0:T(128)S(1)}, u32[]{:S(2)}) copy-start(f32[64]{0:T(128)S(1)} %psum.56) | copy-start | bytes 772
  146.4 256.8 %copy-start.11 = (f32[32]{0:T(128)}, f32[32]{0:T(128)S(1)}, u32[]{:S(2)}) copy-start(f32[32]{0:T(128)S(1)} %fusion.65) | copy-start | bytes 388
  270.6 132.7 %copy-start.12 = (f32[64]{0:T(128)}, f32[64]{0:T(128)S(1)}, u32[]{:S(2)}) copy-start(f32[64]{0:T(128)S(1)} %psum.57) | copy-start | bytes 772
  270.8 132.5 %copy-start.13 = (f32[32]{0:T(128)}, f32[32]{0:T(128)S(1)}, u32[]{:S(2)}) copy-start(f32[32]{0:T(128)S(1)} %fusion.70) | copy-start | bytes 388
  396.2 7.1 copy-start.21
  398.3 14.0 %all-to-all-start = ((bf16[64,1,8]{2,1,0:T(2,128)(2,1)}), bf16[64,1,8]{2,1,0:T(2,128)(2,1)S(1)}, u32[]{:S(2)}, u32[]{:S(2)}) async-start(bf16[64,1,8]{2,1,0:T(2,128)(2,1)} %all_to_all.25), calls=%async_computation | async-start | bytes 65536 | tf_op jit(solution)/shard_map/all_to_all | solution.py:105
  403.3 14.6 %copy-start.4 = (bf16[512,32]{0,1:T(8,128)(2,1)}, bf16[512,32]{0,1:T(8,128)(2,1)S(1)}, u32[]{:S(2)}) copy-start(bf16[512,32]{0,1:T(8,128)(2,1)S(1)} %fusion.41) | copy-start | bytes 98308
  406.3 11.7 copy-start.9
  412.4 56.6 %all-to-all-start.2 = ((bf16[64,8,2048]{2,1,0:T(8,128)(2,1)}), bf16[64,8,2048]{2,1,0:T(8,128)(2,1)}, u32[]{:S(2)}, u32[]{:S(2)}) async-start(bf16[64,8,2048]{2,1,0:T(8,128)(2,1)} %fusion.13), calls=%async_computation.2 | async-start | bytes 4194304 | tf_op jit(solution)/shard_map/all_to_all | solution.py:91
  468.9 57.2 %all-to-all-start.1 = ((bf16[64,8,2048]{2,1,0:T(8,128)(2,1)}), bf16[64,8,2048]{2,1,0:T(8,128)(2,1)}, u32[]{:S(2)}, u32[]{:S(2)}) async-start(bf16[64,8,2048]{2,1,0:T(8,128)(2,1)} %fusion.12), calls=%async_computation.1 | async-start | bytes 4194304 | tf_op jit(solution)/shard_map/all_to_all | solution.py:98
  533.7 22.8 %all-to-all-start.4 = ((bf16[64,1,8]{2,1,0:T(2,128)(2,1)}), bf16[64,1,8]{2,1,0:T(2,128)(2,1)}, u32[]{:S(2)}, u32[]{:S(2)}) async-start(bf16[64,1,8]{2,1,0:T(2,128)(2,1)} %convert_element_type.108), calls=%async_computation.4 | async-start | bytes 65536 | tf_op jit(solution)/shard_map/all_to_all | solution.py:123
  539.9 601.6 %all-reduce.3.cloned.1.call-start = ((), (), s32[]{:S(2)}) async-start(), calls=%async_computation.6 | async-start | bytes 1048576 | tf_op jit(solution)/shard_map/psum | solution.py:170
  539.9 6.2 copy-start.28
  546.1 5.2 copy-start.30
  551.3 401.7 %copy-start.1 = (bf16[2048,64]{0,1:T(8,128)(2,1)S(1)}, bf16[2048,64]{0,1:T(8,128)(2,1)}, u32[]{:S(2)}) copy-start(bf16[2048,64]{0,1:T(8,128)(2,1)} %param.10) | copy-start | bytes 786436
  551.3 401.7 %copy-start.2 = (bf16[1,32,2048]{2,1,0:T(8,128)(2,1)S(1)}, bf16[1,32,2048]{2,1,0:T(8,128)(2,1)}, u32[]{:S(2)}) copy-start(bf16[1,32,2048]{2,1,0:T(8,128)(2,1)} %param.7) | copy-start | bytes 393220
  955.0 189.7 %reduce-scatter.2.cloned.1.call-start = ((), (), s32[]{:S(2)}) async-start(), calls=%async_computation.8 | async-start | bytes 11796480 | tf_op jit(solution)/shard_map/reduce_scatter | solution.py:137
  962.7 3.1 copy-start.27
  962.7 3.1 copy-start.29
  969.0 172.5 %all-to-all-start.3 = ((bf16[64,8,2048]{2,1,0:T(8,128)(2,1)}), bf16[64,8,2048]{2,1,0:T(8,128)(2,1)}, u32[]{:S(2)}, u32[]{:S(2)}) async-start(bf16[64,8,2048]{2,1,0:T(8,128)(2,1)} %fusion.14), calls=%async_computation.3 | async-start | bytes 4194304 | tf_op jit(solution)/shard_map/all_to_all | solution.py:116
  974.6 169.0 %copy-start.7 = (f32[32,64]{1,0:T(8,128)S(1)}, f32[32,64]{1,0:T(8,128)}, u32[]{:S(2)}) copy-start(f32[32,64]{1,0:T(8,128)} %copy-done.6) | copy-start | bytes 24580
  974.6 211.4 %all-reduce.5.cloned.1.call-start = ((), (), s32[]{:S(2)}) async-start(), calls=%async_computation.7 | async-start | bytes 1048576 | tf_op jit(solution)/shard_map/psum | solution.py:170
  (15 other events, 20.4 us)
Sparse Core Ops, SparseCore 0:
  955.1 186.3 all-reduce.2
Sparse Core Ops, SparseCore 1:
  962.8 83.9 reduce-scatter.1
  1141.6 44.4 all-reduce.4
